TPU v7x, 32 devices: a whole 2x2x4 slice. The times are simulated.
32 devices in a mesh: groups: 2 (over x), blk: 16 (over z, y, core).
Axes of the slice: x: 2, y: 2, z: 4, core: 2. Of those that a mesh axis runs over, the one named last changes fastest.
Arguments:
- density: bfloat16 [256, 9, 128, 128], P(('groups', 'blk')), parts along dimension 0, may hold values from -0.25 to 0.25
- ao_values: bfloat16 [384, 4, 128, 256], P(('groups', 'blk')), parts along dimension 0, may hold values from -6 to 6
- kernel: bfloat16 [384, 256, 256], P(('groups', 'blk')), parts along dimension 0, may hold values from -0.375 to 0.375
- grid_weights: float32 [384, 256], P(('groups', 'blk')), parts along dimension 0, may hold values from 0.002 to 0.02
- centre: int32 [384], P(('groups', 'blk')), parts along dimension 0, may hold values from 2 to 125, as said below
- sig_offsets: int32 [384, 4], P(('groups', 'blk')), parts along dimension 0, may hold values from -2 to 2, as said below
- counts: int32 [384], P(('groups', 'blk')), parts along dimension 0, may hold values from 0 to 4, as said below
Outputs:
- exchange: float32 [256, 9, 128, 128], P(('groups', 'blk')), parts along dimension 0
There are 2 independent parts, one for each index of `groups`. A program takes and returns all parts, laid end to end along the dimension named above; each array names one. Nothing has to cross between parts.
Inputs may be any that keep to these rules, and one draw needn't show every extreme that they name: `centre`: the batches in the rows of one blk device have their atom block among that device's 8 blocks; the device's first batch slot has the lowest such block that the range allows, its slot 10 the highest. `sig_offsets`: the 4 offsets of a batch are distinct; those of a device's first slot and of its slot 10 include -2 and 2. `counts`: the first batch slot and slot 10 of each blk device have 4 live blocks and its last slot none.
All inputs are finite; a program needn't handle non-finite values.
Results may differ from a plain program's by a relative error of at most 0.0041.
Values may be sent and summed in bfloat16 or wider, within the bound.
No kernel may reach another device: no remote copies, remote signals or barrier semaphores. Data moves between devices by JAX's collectives and lax.ppermute only.
A program may use at most 128 MiB of HBM per device.

v0:
```python
import functools

import jax
import jax.numpy as jnp
from jax import lax
from jax.experimental import pallas as pl
from jax.experimental.pallas import tpu as pltpu
from jax.sharding import PartitionSpec as P

MIB = 1 << 20
GROUP = 2
LATE_GROUP = 4
LISTS = 7
BUDGET = 44
WAIT = (18, 20)
COST = (10, 7)
SMEM_SPEC = pl.BlockSpec(memory_space=pltpu.SMEM)
VMEM_SPEC = pl.BlockSpec(memory_space=pltpu.VMEM)
ANY_SPEC = pl.BlockSpec(memory_space=pl.ANY)


class Geometry:
    def __init__(self, rows, band, batches, slots):
        self.rows, self.band, self.batches, self.slots = rows, band, batches, slots
        self.half = half = (band - 1) // 2
        self.reach = reach = half // 2
        self.own = rows * band
        low = [(-m, reach + m, band) for m in range(reach, 0, -1)]
        high = [(rows + m, 0, 3 * reach - m) for m in range(reach)]
        self.halo = sum(stop - start for _, start, stop in low)
        low_cut = [half - row for row, _, _ in low]
        high_cut = [rows - row + half for row, _, _ in high]
        early = (
            [(row, cut, stop) for (row, _, stop), cut in zip(low, low_cut)],
            [(row, start, cut) for (row, start, _), cut in zip(high, high_cut)],
        )
        late = (
            [(row, start, cut) for (row, start, _), cut in zip(low, low_cut)],
            [(row, cut, stop) for (row, _, stop), cut in zip(high, high_cut)],
        )
        self.early = sum(stop - start for _, start, stop in early[0])
        self.late = self.halo - self.early
        self.first_at = self.own
        self.early_at = self.own + self.halo
        self.spare = self.early_at + self.early
        cut = 6
        self.pieces = ((0, cut), (cut, self.halo - cut))
        self.halo_base = self.bases((low, high))
        self.early_base = self.bases(early)
        shifts = (rows, -rows)
        self.packs = [self.places(*pair) for pair in zip((low, high), shifts)]
        self.early_packs = [self.places(*pair) for pair in zip(early, shifts)]
        self.late_packs = [self.places(*pair) for pair in zip(late, shifts)]
        self.span = min(2 * reach, rows) * band
        self.quiet = [
            self.others(self.packs[1], 0, self.span),
            self.others(self.packs[0], self.own - self.span, self.own),
        ]
        self.list_size = batches + 2
        self.lengths_at = LISTS * self.list_size
        self.local_at = self.lengths_at + LISTS
        self.count_at = self.local_at + batches
        self.offsets_at = self.count_at + batches
        self.odd_at = self.offsets_at + slots * batches
        self.meta_size = self.odd_at + 1

    def bases(self, sides):
        found = {}
        for segments in sides:
            place = 0
            for row, start, stop in segments:
                found[row] = place - start
                place += stop - start
        return found

    def places(self, segments, shift):
        pack, place = ([], 0)
        for row, start, stop in segments:
            pack.append(((row + shift) * self.band + start, place, stop - start))
            place += stop - start
        return pack

    def others(self, pack, begin, end):
        touched = set()
        for start, _, count in pack:
            touched.update(range(start, start + count))
        runs = []
        for index in range(begin, end):
            if index in touched:
                continue
            if runs and sum(runs[-1]) == index:
                runs[-1] = (runs[-1][0], runs[-1][1] + 1)
            else:
                runs.append((index, 1))
        return runs

    def near_packs(self, piece):
        begin, count = self.pieces[piece]
        found = []
        for pack in self.packs:
            part = []
            for start, place, size in pack:
                low, high = max(place, begin), min(place + size, begin + count)
                if low < high:
                    part.append((start + low - place, low - begin, high - low))
            found.append(part)
        return found

    def pick(self, bases, shift, row, otherwise):
        value = otherwise
        for at, base in bases.items():
            value = jnp.where(row == at, base + shift, value)
        return value


def run_copies(copies):
    for copy in copies:
        copy.start()
    for copy in copies:
        copy.wait()


def by_parity(odd, body, first, second):
    @pl.when(jnp.logical_not(odd))
    def _():
        body(first, second)

    @pl.when(odd)
    def _():
        body(second, first)


CROSS_MANY, CROSS_FEW, NEAR_MANY, NEAR_FEW, INNER_MANY, INNER_FEW, CROSS = range(LISTS)


def build_lists(geo, index, centre_ref, offsets_ref, counts_ref, meta_ref):
    first = index * geo.rows
    odd = index % 2 == 1
    meta_ref[geo.odd_at] = odd.astype(jnp.int32)
    lengths = [jnp.int32(0)] * LISTS
    for b in range(geo.batches):
        local = centre_ref[b] - first
        count = counts_ref[b]
        meta_ref[geo.local_at + b] = local
        meta_ref[geo.count_at + b] = count
        low = high = jnp.bool_(False)
        for k in range(geo.slots):
            offset = offsets_ref[k, b]
            meta_ref[geo.offsets_at + k * geo.batches + b] = offset
            row = local + offset
            low = low | ((k < count) & (row < 0))
            high = high | ((k < count) & (row >= geo.rows))
        cross = (odd & high) | (jnp.logical_not(odd) & low)
        near = (odd & low) | (jnp.logical_not(odd) & high)
        inner = jnp.logical_not(low | high)
        many = count > 2
        few = (count > 0) & jnp.logical_not(many)
        kinds = [kind & size for kind in (cross, near, inner) for size in (many, few)]
        for which, member in enumerate(kinds + [cross]):
            meta_ref[which * geo.list_size + lengths[which]] = b
            lengths[which] = lengths[which] + member.astype(jnp.int32)
    for which in range(LISTS):
        meta_ref[which * geo.list_size + lengths[which]] = geo.batches
        meta_ref[geo.lengths_at + which] = lengths[which]


def zone(geo, odd, cross):
    span = geo.span if cross else geo.own - geo.span
    return pl.ds(jnp.where(odd == cross, geo.own - span, 0), span)


def pack_kernel(
    geo, density_ref, centre_in, offsets_in, counts_in,
    near_ref, cross_ref, meta_ref, acc_ref,
    centre_ref, offsets_ref, counts_ref, sems,
):
    index = lax.axis_index("blk")
    odd = index % 2 == 1

    def copies(up, down):
        return [
            pltpu.make_async_copy(
                density_ref.at[pl.ds(start, count)], ref.at[pl.ds(place, count)], sems.at[side, i]
            )
            for side, (pack, ref) in enumerate(zip(geo.packs, (up, down)))
            for i, (start, place, count) in enumerate(pack)
        ]

    def start(up, down):
        for copy in copies(up, down):
            copy.start()

    by_parity(odd, start, near_ref, cross_ref)
    scalars = [
        pltpu.make_async_copy(*pair, sems.at[2, i])
        for i, pair in enumerate(
            ((centre_in, centre_ref), (offsets_in, offsets_ref), (counts_in, counts_ref))
        )
    ]
    for copy in scalars:
        copy.start()
    for where in (zone(geo, odd, False), pl.ds(geo.first_at, geo.halo)):
        acc_ref[where] = jnp.zeros_like(acc_ref[where])
    for copy in scalars:
        copy.wait()
    build_lists(geo, index, centre_ref, offsets_ref, counts_ref, meta_ref)
    for copy in copies(near_ref, cross_ref):
        copy.wait()


def group_count(geo, meta_ref, which):
    return (meta_ref[geo.lengths_at + which] + GROUP - 1) // GROUP


def waits():
    return (lax.axis_index("blk") + 1) // 2 % 2 == 1


def inner_share(geo, meta_ref):
    before = BUDGET
    for which in (CROSS_MANY, CROSS_FEW, NEAR_MANY, NEAR_FEW):
        before = before - COST[which % 2] * group_count(geo, meta_ref, which)
    odd = meta_ref[geo.odd_at] == 1
    waiting = jnp.where(waits(), jnp.where(odd, WAIT[1], WAIT[0]), 0)
    share = []
    for which in (INNER_MANY, INNER_FEW):
        cost, count = COST[which % 2], group_count(geo, meta_ref, which)
        first = jnp.minimum(jnp.maximum(before, 0) // cost, count)
        second = jnp.minimum(jnp.maximum(waiting, 0) // cost, count - first)
        before = before - cost * first
        waiting = waiting - cost * second
        share.append((0, first, first + second, count))
    return share


def inner_part(geo, meta_ref, stage, refs):
    for which, width, bounds in zip(
        (INNER_MANY, INNER_FEW), (geo.slots, 2), inner_share(geo, meta_ref)
    ):
        each_group(
            geo,
            meta_ref,
            which,
            lambda chosen, width=width: add_whole(geo, chosen, width, *refs),
            begin=bounds[stage],
            end=bounds[stage + 1],
        )


def each_group(geo, meta_ref, which, body, size=GROUP, begin=0, end=None):
    length = meta_ref[geo.lengths_at + which]

    def step(i, carry):
        chosen = []
        for n in range(size):
            place = i * size + n
            there = place < length
            b = meta_ref[which * geo.list_size + jnp.minimum(place, length)]
            chosen.append((jnp.where(there, b, 0), there))
        body(chosen)
        return carry

    lax.fori_loop(begin, (length + size - 1) // size if end is None else end, step, 0)


class Slots:
    def __init__(self, geo, meta_ref, b, there, width):
        local = meta_ref[geo.local_at + b]
        count = jnp.where(there, meta_ref[geo.count_at + b], 0)
        self.offset = [meta_ref[geo.offsets_at + k * geo.batches + b] for k in range(width)]
        self.local = local
        self.row = [local + offset for offset in self.offset]
        self.live = [k < count for k in range(width)]
        self.own = [(row >= 0) & (row < geo.rows) for row in self.row]
        self.width = width


def panels(slots, ao_ref, b):
    return jnp.concatenate(
        [
            ao_ref[b, k] * jnp.where(slots.live[k], 1.0, 0.0).astype(ao_ref.dtype)
            for k in range(slots.width)
        ],
        axis=0,
    )


def gathered(tiles_ref, places):
    return jnp.concatenate(
        [jnp.concatenate([tiles_ref[place] for place in row], axis=1) for row in places], axis=0
    )


def potentials(xs, tiles, batches, kernel_ref):
    fs = [
        jnp.dot(t, x, preferred_element_type=jnp.float32).astype(jnp.bfloat16)
        for t, x in zip(tiles, xs)
    ]
    return [
        jnp.dot(f, kernel_ref[b], preferred_element_type=jnp.float32) for f, b in zip(fs, batches)
    ]


def outer_product(x, h):
    return lax.dot_general(x, h, (((1,), (1,)), ((), ())), preferred_element_type=jnp.float32)


def chain(xs, tiles, batches, kernel_ref, weights_ref):
    gs = potentials(xs, tiles, batches, kernel_ref)
    hs = [(g * weights_ref[pl.ds(b, 1), :]).astype(jnp.bfloat16) for g, b in zip(gs, batches)]
    return [outer_product(x, h) for x, h in zip(xs, hs)]


def scatter(part, target, nb, acc_ref):
    for k, row in enumerate(target):
        for j, place in enumerate(row):
            acc_ref[place] += part[k * nb : (k + 1) * nb, j * nb : (j + 1) * nb]


def add_whole(
    geo, chosen, width, meta_ref, tiles_ref, ao_ref, kernel_ref, weights_ref, acc_ref, halo_ref=None
):
    xs, tiles, targets = ([], [], [])
    for b, there in chosen:
        slots = Slots(geo, meta_ref, b, there, width)
        xs.append(panels(slots, ao_ref, b))
        rows, target = ([], [])
        for k in range(width):
            band = [slots.offset[j] - slots.offset[k] + geo.half for j in range(width)]
            own = slots.own[k]
            base = jnp.where(slots.live[k] & own, slots.row[k], 0) * geo.band
            row = jnp.concatenate([tiles_ref[base + o] for o in band], axis=1)
            if halo_ref is not None:
                away = slots.live[k] & jnp.logical_not(own)
                outside = jnp.where(away, geo.pick(geo.halo_base, 0, slots.row[k], 0), 0)
                other = [halo_ref[jnp.where(away, outside + o, 0)] for o in band]
                row = jnp.where(away, jnp.concatenate(other, axis=1), row)
                base = jnp.where(away, outside + geo.first_at, base)
            rows.append(row)
            target.append(
                [
                    jnp.where(slots.live[k] & slots.live[j], base + band[j], geo.spare)
                    for j in range(width)
                ]
            )
        tiles.append(jnp.concatenate(rows, axis=0))
        targets.append(target)
    parts = chain(xs, tiles, [b for b, _ in chosen], kernel_ref, weights_ref)
    for part, target in zip(parts, targets):
        scatter(part, target, ao_ref.shape[2], acc_ref)


def add_own(geo, chosen, width, meta_ref, tiles_ref, ao_ref, kernel_ref, weights_ref, acc_ref):
    xs, tiles, targets = ([], [], [])
    for b, there in chosen:
        slots = Slots(geo, meta_ref, b, there, width)
        xs.append(panels(slots, ao_ref, b))
        places, target = ([], [])
        for k in range(width):
            row = slots.row[k]
            band = [slots.offset[j] - slots.offset[k] + geo.half for j in range(width)]
            base = jnp.where(slots.own[k], row, 0) * geo.band
            places.append([base + o for o in band])
            base = geo.pick(geo.early_base, geo.early_at, row, base)
            target.append(
                [
                    jnp.where(
                        slots.live[k] & slots.live[j] & slots.own[j], base + band[j], geo.spare
                    )
                    for j in range(width)
                ]
            )
        tiles.append(gathered(tiles_ref, places))
        targets.append(target)
    parts = chain(xs, tiles, [b for b, _ in chosen], kernel_ref, weights_ref)
    for part, target in zip(parts, targets):
        scatter(part, target, ao_ref.shape[2], acc_ref)


def halo_rows(geo, meta_ref, slots):
    odd = meta_ref[geo.odd_at] == 1
    rows, places, present = ([], [], [])
    for i in range(geo.reach):
        row = jnp.where(odd, geo.rows + i, i - geo.reach)
        place, found = (jnp.int32(0), jnp.bool_(False))
        for k in range(slots.width):
            hit = slots.live[k] & (slots.row[k] == row)
            place = jnp.where(hit, k, place)
            found = found | hit
        rows.append(row)
        places.append(place)
        present.append(found)
    return rows, places, present


def add_corner(geo, chosen, meta_ref, halo_ref, ao_ref, kernel_ref, weights_ref, h_ref, total_ref):
    nb = ao_ref.shape[2]
    factor = lambda flag: jnp.where(flag, 1.0, 0.0)
    xs, sides, tiles, masks = ([], [], [], [])
    for b, there in chosen:
        slots = Slots(geo, meta_ref, b, there, geo.slots)
        rows, places, present = halo_rows(geo, meta_ref, slots)
        xs.append(panels(slots, ao_ref, b))
        sides.append(
            jnp.concatenate(
                [
                    ao_ref[b, place] * factor(found).astype(ao_ref.dtype)
                    for place, found in zip(places, present)
                ],
                axis=0,
            )
        )
        picked = []
        for row, found in zip(rows, present):
            base = geo.pick(geo.halo_base, 0, row, 0) - row + geo.half
            picked.append([jnp.where(found, base + column, 0) for column in slots.row])
        tiles.append(gathered(halo_ref, picked))
        masks.append([factor(found) for found in present])
    gs = potentials(xs, tiles, [b for b, _ in chosen], kernel_ref)
    hs = []
    for g, mask, (b, there) in zip(gs, masks, chosen):
        weights = weights_ref[pl.ds(b, 1), :]
        h = jnp.concatenate(
            [g[i * nb : (i + 1) * nb] * (weights * mask[i]) for i in range(geo.reach)], axis=0
        ).astype(jnp.bfloat16)
        h_ref[jnp.where(there, b, geo.batches)] = h
        hs.append(h)
    total_ref[...] += outer_product(
        jnp.concatenate(sides, axis=1), jnp.concatenate(hs, axis=1)
    )


def add_columns(geo, chosen, width, meta_ref, ao_ref, h_ref, acc_ref):
    parts, targets = ([], [])
    for b, there in chosen:
        slots = Slots(geo, meta_ref, b, there, width)
        rows, _, present = halo_rows(geo, meta_ref, slots)
        parts.append(outer_product(ao_ref[b, pl.ds(0, width)].reshape(-1, ao_ref.shape[3]), h_ref[b]))
        targets.append(
            [
                [
                    jnp.where(
                        slots.live[k] & slots.own[k] & found,
                        slots.row[k] * geo.band + row - slots.row[k] + geo.half,
                        geo.spare,
                    )
                    for row, found in zip(rows, present)
                ]
                for k in range(width)
            ]
        )
    for part, target in zip(parts, targets):
        scatter(part, target, ao_ref.shape[2], acc_ref)


def early_kernel(
    geo, meta_ref, tiles_ref, ao_ref, kernel_ref, weights_ref, acc_in, acc_ref
):
    odd = meta_ref[geo.odd_at] == 1
    for where in (zone(geo, odd, True), pl.ds(geo.early_at, geo.early), pl.ds(geo.spare, 1)):
        acc_ref[where] = jnp.zeros_like(acc_ref[where])
    refs = (meta_ref, tiles_ref, ao_ref, kernel_ref, weights_ref, acc_ref)
    for which, width in ((CROSS_MANY, geo.slots), (CROSS_FEW, 2)):
        each_group(
            geo, meta_ref, which, lambda chosen, width=width: add_own(geo, chosen, width, *refs)
        )


def near_kernel(
    geo, meta_ref, halo_ref, tiles_ref, ao_ref, kernel_ref, weights_ref, acc_in, acc_ref,
    early_out, *outs,
):
    early_out[...] = acc_ref[pl.ds(geo.early_at, geo.early)].astype(early_out.dtype)
    refs = (meta_ref, tiles_ref, ao_ref, kernel_ref, weights_ref, acc_ref, halo_ref)
    for which, width in ((NEAR_MANY, geo.slots), (NEAR_FEW, 2)):
        each_group(
            geo, meta_ref, which, lambda chosen, width=width: add_whole(geo, chosen, width, *refs)
        )
    for out, (start, count) in zip(outs, geo.pieces):
        out[...] = acc_ref[pl.ds(geo.first_at + start, count)].astype(out.dtype)
    inner_part(geo, meta_ref, 0, refs[:-1])


def waiting_kernel(
    geo, meta_ref, tiles_ref, ao_ref, kernel_ref, weights_ref, acc_in, acc_ref, done_ref
):
    inner_part(geo, meta_ref, 1, (meta_ref, tiles_ref, ao_ref, kernel_ref, weights_ref, acc_ref))
    done_ref[0] = 1


def late_kernel(
    geo, meta_ref, done_ref, halo_ref, ao_ref, kernel_ref, weights_ref, h_ref, late_out, total_ref
):
    nb = ao_ref.shape[2]
    total_ref[...] = jnp.zeros_like(total_ref)

    def work(chosen):
        add_corner(
            geo, chosen, meta_ref, halo_ref, ao_ref, kernel_ref, weights_ref, h_ref, total_ref
        )

    groups = (meta_ref[geo.lengths_at + CROSS] + 1) // LATE_GROUP
    each_group(geo, meta_ref, CROSS, work, size=LATE_GROUP, end=groups)
    each_group(geo, meta_ref, CROSS, work, size=LATE_GROUP // 2, begin=2 * groups)
    for i in range(geo.reach):
        for j in range(geo.reach):
            late_out[i * geo.reach + j] = total_ref[
                i * nb : (i + 1) * nb, j * nb : (j + 1) * nb
            ].astype(late_out.dtype)


def inner_kernel(
    geo, meta_ref, first_a, first_b, tiles_ref, ao_ref, kernel_ref, weights_ref, h_ref, acc_in,
    acc_ref, out_ref, sems,
):
    odd = meta_ref[geo.odd_at] == 1
    refs = (meta_ref, tiles_ref, ao_ref, kernel_ref, weights_ref, acc_ref)
    inner_part(geo, meta_ref, 2, refs)

    def add_near(up, down):
        for piece, ref in enumerate((first_a, first_b)):
            for start, place, count in geo.near_packs(piece)[0 if up else 1]:
                acc_ref[pl.ds(start, count)] += ref[pl.ds(place, count)].astype(jnp.float32)

    by_parity(odd, add_near, True, False)
    done = zone(geo, odd, False)
    copy = pltpu.make_async_copy(acc_ref.at[done], out_ref.at[done], sems.at[0])
    copy.start()
    for which, width in ((CROSS_MANY, geo.slots), (CROSS_FEW, 2)):
        each_group(
            geo,
            meta_ref,
            which,
            lambda chosen, width=width: add_columns(
                geo, chosen, width, meta_ref, ao_ref, h_ref, acc_ref
            ),
        )

    def write_quiet(up, down):
        run_copies(
            [
                pltpu.make_async_copy(
                    acc_ref.at[pl.ds(start, count)], out_ref.at[pl.ds(start, count)], sems.at[1 + i]
                )
                for i, (start, count) in enumerate(geo.quiet[0 if up else 1])
            ]
        )

    by_parity(odd, write_quiet, True, False)
    copy.wait()


def finish_cross(geo, odd, parts, acc_ref, out_ref, total, sems):
    def add(up, down):
        copies = []
        for packs, ref in parts:
            for start, place, count in packs[0 if up else 1]:
                spot = pl.ds(len(copies) * geo.band, count)
                total[spot] = acc_ref[pl.ds(start, count)] + ref[pl.ds(place, count)].astype(
                    jnp.float32
                )
                copy = pltpu.make_async_copy(
                    total.at[spot], out_ref.at[pl.ds(start, count)], sems.at[len(copies)]
                )
                copy.start()
                copies.append(copy)
        for copy in copies:
            copy.wait()

    by_parity(odd, add, False, True)


def has_time(geo, meta_ref):
    left = [bounds[3] - bounds[2] for bounds in inner_share(geo, meta_ref)]
    return waits() & (left[0] + left[1] == 0)


def early_join_kernel(geo, meta_ref, early_ref, acc_ref, out_in, out_ref, total, sems):
    @pl.when(has_time(geo, meta_ref))
    def _():
        odd = meta_ref[geo.odd_at] == 1
        finish_cross(geo, odd, ((geo.early_packs, early_ref),), acc_ref, out_ref, total, sems)


def finish_kernel(geo, meta_ref, late_ref, early_ref, acc_ref, out_in, out_ref, total, sems):
    odd = meta_ref[geo.odd_at] == 1
    late = (geo.late_packs, late_ref)
    joined = has_time(geo, meta_ref)

    @pl.when(joined)
    def _():
        finish_cross(geo, odd, (late,), acc_ref, out_ref, total, sems)

    @pl.when(jnp.logical_not(joined))
    def _():
        parts = ((geo.early_packs, early_ref), late)
        finish_cross(geo, odd, parts, acc_ref, out_ref, total, sems)


def call(kernel, out_shape, in_specs, out_specs, scratch, aliases=None, cost=None):
    return pl.pallas_call(
        kernel,
        out_shape=out_shape,
        in_specs=in_specs,
        out_specs=out_specs,
        scratch_shapes=scratch,
        input_output_aliases=aliases or {},
        cost_estimate=cost,
        compiler_params=pltpu.CompilerParams(vmem_limit_bytes=16 * MIB),
    )


def to_first(x, size):
    pairs = [(i, i + 1) for i in range(0, size - 1, 2)]
    got = lax.ppermute(x, "blk", pairs + [(j, i) for i, j in pairs])
    return pltpu.with_memory_space_constraint(got, pltpu.VMEM)


def to_second(x, size):
    pairs = [(i, i + 1) for i in range(1, size - 1, 2)]
    got = lax.ppermute(x, "blk", pairs + [(j, i) for i, j in pairs])
    return pltpu.with_memory_space_constraint(got, pltpu.VMEM)


def local(density, ao_values, kernel, grid_weights, centre, sig_offsets, counts):
    rows, band, nb, _ = density.shape
    batches, slots, _, pts = ao_values.shape
    size = lax.axis_size("blk")
    geo = Geometry(rows, band, batches, slots)
    in_hbm = lambda x: pltpu.with_memory_space_constraint(x, pltpu.HBM)
    tiles = density.reshape(geo.own, nb, nb)
    pack = lambda count: pltpu.VMEM((count, nb, nb), jnp.bfloat16)
    dma = pltpu.SemaphoreType.DMA
    acc_type = pltpu.VMEM((geo.spare + 1, nb, nb), jnp.float32)

    near_halo, cross_halo, meta, acc = call(
        functools.partial(pack_kernel, geo),
        (pack(geo.halo),) * 2 + (pltpu.SMEM((geo.meta_size,), jnp.int32), acc_type),
        [ANY_SPEC] * 4,
        (VMEM_SPEC,) * 2 + (SMEM_SPEC, VMEM_SPEC),
        [
            pltpu.SMEM((batches,), jnp.int32),
            pltpu.SMEM((slots, batches), jnp.int32),
            pltpu.SMEM((batches,), jnp.int32),
            dma((3, max(geo.reach, 3))),
        ],
        cost=pl.CostEstimate(flops=10**10, bytes_accessed=10**8, transcendentals=0),
    )(in_hbm(tiles), in_hbm(centre), in_hbm(sig_offsets.T), in_hbm(counts))
    cross_halo = to_second(cross_halo, size)
    near_halo = to_first(near_halo, size)

    panel = (tiles, ao_values, kernel, grid_weights)
    acc = call(
        functools.partial(early_kernel, geo),
        acc_type,
        [SMEM_SPEC] + [VMEM_SPEC] * 5,
        VMEM_SPEC,
        [],
        {5: 0},
    )(meta, *panel, acc)

    acc, early, *first = call(
        functools.partial(near_kernel, geo),
        (acc_type, pack(geo.early)) + tuple(pack(count) for _, count in geo.pieces),
        [SMEM_SPEC] + [VMEM_SPEC] * 6,
        (VMEM_SPEC,) * 4,
        [],
        {6: 0},
    )(meta, near_halo, *panel, acc)
    early = to_second(early, size)
    first = [to_first(piece, size) for piece in first]

    acc, done = call(
        functools.partial(waiting_kernel, geo),
        (acc_type, pltpu.SMEM((1,), jnp.int32)),
        [SMEM_SPEC] + [VMEM_SPEC] * 5,
        (VMEM_SPEC, SMEM_SPEC),
        [],
        {5: 0},
    )(meta, *panel, acc)

    h_type = pltpu.VMEM((batches + 1, geo.reach * nb, pts), jnp.bfloat16)
    h, late = call(
        functools.partial(late_kernel, geo),
        (h_type, pack(geo.late)),
        [SMEM_SPEC] * 2 + [VMEM_SPEC] * 4,
        (VMEM_SPEC,) * 2,
        [pltpu.VMEM((geo.reach * nb, geo.reach * nb), jnp.float32)],
    )(meta, done, cross_halo, *panel[1:])
    late = to_second(late, size)

    whole = jax.ShapeDtypeStruct((geo.own, nb, nb), jnp.float32)
    acc, out = call(
        functools.partial(inner_kernel, geo),
        (acc_type, whole),
        [SMEM_SPEC] + [VMEM_SPEC] * 8,
        (VMEM_SPEC, ANY_SPEC),
        [dma((1 + max(len(runs) for runs in geo.quiet),))],
        {8: 0},
    )(meta, *first, *panel, h, acc)

    for kernel_of, got, parts in (
        (early_join_kernel, (early,), geo.reach),
        (finish_kernel, (late, early), 2 * geo.reach),
    ):
        out = call(
            functools.partial(kernel_of, geo),
            whole,
            [SMEM_SPEC] + [VMEM_SPEC] * (len(got) + 1) + [ANY_SPEC],
            ANY_SPEC,
            [pltpu.VMEM((parts * band, nb, nb), jnp.float32), dma((parts,))],
            {len(got) + 2: 0},
        )(meta, *got, acc, out)
    return out.reshape(rows, band, nb, nb)


def solution(mesh):
    placed = (
        P(("groups", "blk"), None, None, None),
        P(("groups", "blk"), None, None, None),
        P(("groups", "blk"), None, None),
        P(("groups", "blk"), None),
        P(("groups", "blk")),
        P(("groups", "blk"), None),
        P(("groups", "blk")),
    )
    return jax.shard_map(
        local,
        mesh=mesh,
        in_specs=placed,
        out_specs=P(("groups", "blk"), None, None, None),
        check_vma=False,
    )
```

profile of v0, /device:TPU:19, one launch (start us, length us, event | category | flops | bytes accessed | tf_op | source)
XLA Modules:
  0.0 25.2 jit_solution(16215737581716507574)
XLA Ops:
  0.0 0.0 copy-start
  0.0 0.0 copy-start.1
  0.0 0.0 copy-start.2
  0.0 0.0 copy-start.3
  0.0 1.4 %shard_map.73 = (bf16[11,128,128]{2,1,0:T(8,128)(2,1)S(1)}, bf16[11,128,128]{2,1,0:T(8,128)(2,1)S(1)}, s32[178]{0:T(256)S(4)}, f32[91,128,128]{2,1,0:T(8,128)S(1)}) custom-call(bf16[72,128,128]{2,1,0:T(8,128)(2,1)} %bitcast.3, s32[12]{0:T(128)} %centre_in.1, s32[4,12]{1,0:T(4,128)} %bitcast.8, s32[12]{0:T(128)} %counts_in.1), custom_call_target="tpu_custom_call" | custom-call | flops 10000000000 | bytes 100000000 | tf_op jit(solution)/shard_map/pallas_call | solution.py:636
  1.5 0.7 %collective-permute-start = (bf16[11,128,128]{2,1,0:T(8,128)(2,1)S(1)}, bf16[11,128,128]{2,1,0:T(8,128)(2,1)S(1)}, u32[]{:S(2)}, u32[]{:S(2)}) collective-permute-start(bf16[11,128,128]{2,1,0:T(8,128)(2,1)S(1)} %get-tuple-element.20), channel_id=1, source_target_pairs={{0,1},{2,3},{4,5},{6,7},{8,9},{10,11},{12,13},{14,15},{1,0},{3,2},... | collective-permute-start | bytes 1081352 | tf_op jit(solution)/shard_map/ppermute | solution.py:615
  2.2 3.3 %collective-permute-start.1 = (bf16[11,128,128]{2,1,0:T(8,128)(2,1)S(1)}, bf16[11,128,128]{2,1,0:T(8,128)(2,1)S(1)}, u32[]{:S(2)}, u32[]{:S(2)}) collective-permute-start(bf16[11,128,128]{2,1,0:T(8,128)(2,1)S(1)} %get-tuple-element.24), channel_id=1, source_target_pairs={{1,2},{3,4},{5,6},{7,8},{9,10},{11,12},{13,14},{2,1},{4,3},{6,5},{... | collective-permute-start | bytes 1081352 | tf_op jit(solution)/shard_map/ppermute | solution.py:621
  5.5 0.0 copy-done
  5.5 0.0 copy-done.1
  5.5 0.0 copy-done.2
  5.5 0.0 copy-done.3
  5.5 1.2 %shard_map.74.acc_in = f32[91,128,128]{2,1,0:T(8,128)S(1)} custom-call(s32[178]{0:T(256)S(4)} %get-tuple-element.19.meta_ref, bf16[72,128,128]{2,1,0:T(8,128)(2,1)S(1)} %bitcast.4, bf16[12,4,128,256]{3,2,1,0:T(8,128)(2,1)S(1)} %copy-done, bf16[12,256,256]{2,1,0:T(8,128)(2,1)S(1)} %copy-done.1, ...), custom_call_target="tpu_custom_call", output_to_operand_aliasing={{}: (5, {})} | custom-call | tf_op jit(solution)/shard_map/pallas_call | solution.py:653
  6.8 0.0 collective-permute-done.halo_ref
  6.8 3.1 %shard_map.75 = (f32[91,128,128]{2,1,0:T(8,128)S(1)}, bf16[7,128,128]{2,1,0:T(8,128)(2,1)S(1)}, bf16[6,128,128]{2,1,0:T(8,128)(2,1)S(1)}, bf16[5,128,128]{2,1,0:T(8,128)(2,1)S(1)}) custom-call(s32[178]{0:T(256)S(4)} %get-tuple-element.19.meta_ref, bf16[11,128,128]{2,1,0:T(8,128)(2,1)S(1)} %collective-permute-done.halo_ref, ...), custom_call_target="tpu_custom_call", output_to_operand_aliasing={{0}: (6, {})} | custom-call | tf_op jit(solution)/shard_map/pallas_call | solution.py:662
  9.9 2.6 %collective-permute-start.3 = (bf16[7,128,128]{2,1,0:T(8,128)(2,1)S(1)}, bf16[7,128,128]{2,1,0:T(8,128)(2,1)S(1)}, u32[]{:S(2)}, u32[]{:S(2)}) collective-permute-start(bf16[7,128,128]{2,1,0:T(8,128)(2,1)S(1)} %get-tuple-element.26), channel_id=1, source_target_pairs={{1,2},{3,4},{5,6},{7,8},{9,10},{11,12},{13,14},{2,1},{4,3},{6,5},{... | collective-permute-start | bytes 688136 | tf_op jit(solution)/shard_map/ppermute | solution.py:621
  12.5 1.1 %collective-permute-start.4 = (bf16[6,128,128]{2,1,0:T(8,128)(2,1)S(1)}, bf16[6,128,128]{2,1,0:T(8,128)(2,1)S(1)}, u32[]{:S(2)}, u32[]{:S(2)}) collective-permute-start(bf16[6,128,128]{2,1,0:T(8,128)(2,1)S(1)} %get-tuple-element.27), channel_id=1, source_target_pairs={{0,1},{2,3},{4,5},{6,7},{8,9},{10,11},{12,13},{14,15},{1,0},{3,2},... | collective-permute-start | bytes 589832 | tf_op jit(solution)/shard_map/ppermute | solution.py:615
  13.6 0.1 collective-permute-start.5
  13.7 3.7 %collective-permute-done.1.halo_ref = bf16[11,128,128]{2,1,0:T(8,128)(2,1)S(1)} collective-permute-done((bf16[11,128,128]{2,1,0:T(8,128)(2,1)S(1)}, bf16[11,128,128]{2,1,0:T(8,128)(2,1)S(1)}, u32[]{:S(2)}, u32[]{:S(2)}) %collective-permute-start.1) | collective-permute-done | bytes 360480 | tf_op jit(solution)/shard_map/ppermute | solution.py:621
  17.4 0.7 %shard_map.77 = (bf16[13,256,256]{2,1,0:T(8,128)(2,1)S(1)}, bf16[4,128,128]{2,1,0:T(8,128)(2,1)S(1)}) custom-call(s32[178]{0:T(256)S(4)} %get-tuple-element.19.meta_ref, s32[1]{0:T(128)S(4)} %get-tuple-element.23.done_ref, bf16[11,128,128]{2,1,0:T(8,128)(2,1)S(1)} %collective-permute-done.1.halo_ref, bf16[12,4,128,256]{3,2,1,0:T(8,128)(2,1)S(1)} %copy-done, ...), custom_call_target="tpu_custom_call" | custom-call | tf_op jit(solution)/shard_map/pallas_call | solution.py:683
  18.1 1.9 %collective-permute-start.2 = (bf16[4,128,128]{2,1,0:T(8,128)(2,1)S(1)}, bf16[4,128,128]{2,1,0:T(8,128)(2,1)S(1)}, u32[]{:S(2)}, u32[]{:S(2)}) collective-permute-start(bf16[4,128,128]{2,1,0:T(8,128)(2,1)S(1)} %get-tuple-element.25), channel_id=1, source_target_pairs={{1,2},{3,4},{5,6},{7,8},{9,10},{11,12},{13,14},{2,1},{4,3},{6,5},{... | collective-permute-start | bytes 393224 | tf_op jit(solution)/shard_map/ppermute | solution.py:621
  20.1 0.0 collective-permute-done.5.first_b
  20.1 0.0 collective-permute-done.4.first_a
  20.1 2.1 %shard_map.78 = (f32[91,128,128]{2,1,0:T(8,128)S(1)}, f32[72,128,128]{2,1,0:T(8,128)}) custom-call(s32[178]{0:T(256)S(4)} %get-tuple-element.19.meta_ref, bf16[6,128,128]{2,1,0:T(8,128)(2,1)S(1)} %collective-permute-done.4.first_a, bf16[5,128,128]{2,1,0:T(8,128)(2,1)S(1)} %collective-permute-done.5.first_b, ...), custom_call_target="tpu_custom_call", output_to_operand_aliasing={{0}: (8, {})} | custom-call | tf_op jit(solution)/shard_map/pallas_call | solution.py:693
  22.2 0.0 collective-permute-done.3.early_ref
  22.2 0.9 %shard_map.79.out_in = f32[72,128,128]{2,1,0:T(8,128)} custom-call(s32[178]{0:T(256)S(4)} %get-tuple-element.19.meta_ref, bf16[7,128,128]{2,1,0:T(8,128)(2,1)S(1)} %collective-permute-done.3.early_ref, f32[91,128,128]{2,1,0:T(8,128)S(1)} %get-tuple-element.31.acc_ref, f32[72,128,128]{2,1,0:T(8,128)} %get-tuple-element.32.out_in), custom_call_target="tpu_custom_call", output_to_operand_aliasing={{}: (3, {})} | custom-call | tf_op jit(solution)/shard_map/pallas_call | solution.py:706
  23.1 1.3 %collective-permute-done.2.late_ref = bf16[4,128,128]{2,1,0:T(8,128)(2,1)S(1)} collective-permute-done((bf16[4,128,128]{2,1,0:T(8,128)(2,1)S(1)}, bf16[4,128,128]{2,1,0:T(8,128)(2,1)S(1)}, u32[]{:S(2)}, u32[]{:S(2)}) %collective-permute-start.2) | collective-permute-done | bytes 131104 | tf_op jit(solution)/shard_map/ppermute | solution.py:621
  24.4 0.7 %shard_map.80 = f32[72,128,128]{2,1,0:T(8,128)} custom-call(s32[178]{0:T(256)S(4)} %get-tuple-element.19.meta_ref, bf16[4,128,128]{2,1,0:T(8,128)(2,1)S(1)} %collective-permute-done.2.late_ref, bf16[7,128,128]{2,1,0:T(8,128)(2,1)S(1)} %collective-permute-done.3.early_ref, ...), custom_call_target="tpu_custom_call", output_to_operand_aliasing={{}: (4, {})} | custom-call | tf_op jit(solution)/shard_map/pallas_call | solution.py:706
  (1 shorter events, 0.0 us)
Async XLA Ops:
  0.0 5.5 %copy-start = (bf16[12,4,128,256]{3,2,1,0:T(8,128)(2,1)S(1)}, bf16[12,4,128,256]{3,2,1,0:T(8,128)(2,1)}, u32[]{:S(2)}) copy-start(bf16[12,4,128,256]{3,2,1,0:T(8,128)(2,1)} %ao_ref.9) | copy-start | bytes 9437188
  0.0 5.5 %copy-start.1 = (bf16[12,256,256]{2,1,0:T(8,128)(2,1)S(1)}, bf16[12,256,256]{2,1,0:T(8,128)(2,1)}, u32[]{:S(2)}) copy-start(bf16[12,256,256]{2,1,0:T(8,128)(2,1)} %kernel_ref.9) | copy-start | bytes 4718596
  0.0 5.5 %copy-start.2 = (bf16[8,9,128,128]{3,2,1,0:T(8,128)(2,1)S(1)}, bf16[8,9,128,128]{3,2,1,0:T(8,128)(2,1)}, u32[]{:S(2)}) copy-start(bf16[8,9,128,128]{3,2,1,0:T(8,128)(2,1)} %param.7) | copy-start | bytes 7077892
  0.0 5.5 %copy-start.3 = (f32[12,256]{1,0:T(8,128)S(1)}, f32[12,256]{1,0:T(8,128)}, u32[]{:S(2)}) copy-start(f32[12,256]{1,0:T(8,128)} %weights_ref.9) | copy-start | bytes 36868
  1.5 5.3 %collective-permute-start = (bf16[11,128,128]{2,1,0:T(8,128)(2,1)S(1)}, bf16[11,128,128]{2,1,0:T(8,128)(2,1)S(1)}, u32[]{:S(2)}, u32[]{:S(2)}) collective-permute-start(bf16[11,128,128]{2,1,0:T(8,128)(2,1)S(1)} %get-tuple-element.20), channel_id=1, source_target_pairs={{0,1},{2,3},{4,5},{6,7},{8,9},{10,11},{12,13},{14,15},{1,0},{3,2},... | collective-permute-start | bytes 1081352 | tf_op jit(solution)/shard_map/ppermute | solution.py:615
  2.2 15.2 %collective-permute-start.1 = (bf16[11,128,128]{2,1,0:T(8,128)(2,1)S(1)}, bf16[11,128,128]{2,1,0:T(8,128)(2,1)S(1)}, u32[]{:S(2)}, u32[]{:S(2)}) collective-permute-start(bf16[11,128,128]{2,1,0:T(8,128)(2,1)S(1)} %get-tuple-element.24), channel_id=1, source_target_pairs={{1,2},{3,4},{5,6},{7,8},{9,10},{11,12},{13,14},{2,1},{4,3},{6,5},{... | collective-permute-start | bytes 1081352 | tf_op jit(solution)/shard_map/ppermute | solution.py:621
  9.9 12.3 %collective-permute-start.3 = (bf16[7,128,128]{2,1,0:T(8,128)(2,1)S(1)}, bf16[7,128,128]{2,1,0:T(8,128)(2,1)S(1)}, u32[]{:S(2)}, u32[]{:S(2)}) collective-permute-start(bf16[7,128,128]{2,1,0:T(8,128)(2,1)S(1)} %get-tuple-element.26), channel_id=1, source_target_pairs={{1,2},{3,4},{5,6},{7,8},{9,10},{11,12},{13,14},{2,1},{4,3},{6,5},{... | collective-permute-start | bytes 688136 | tf_op jit(solution)/shard_map/ppermute | solution.py:621
  12.5 7.6 %collective-permute-start.4 = (bf16[6,128,128]{2,1,0:T(8,128)(2,1)S(1)}, bf16[6,128,128]{2,1,0:T(8,128)(2,1)S(1)}, u32[]{:S(2)}, u32[]{:S(2)}) collective-permute-start(bf16[6,128,128]{2,1,0:T(8,128)(2,1)S(1)} %get-tuple-element.27), channel_id=1, source_target_pairs={{0,1},{2,3},{4,5},{6,7},{8,9},{10,11},{12,13},{14,15},{1,0},{3,2},... | collective-permute-start | bytes 589832 | tf_op jit(solution)/shard_map/ppermute | solution.py:615
  13.6 6.4 %collective-permute-start.5 = (bf16[5,128,128]{2,1,0:T(8,128)(2,1)S(1)}, bf16[5,128,128]{2,1,0:T(8,128)(2,1)S(1)}, u32[]{:S(2)}, u32[]{:S(2)}) collective-permute-start(bf16[5,128,128]{2,1,0:T(8,128)(2,1)S(1)} %get-tuple-element.28), channel_id=1, source_target_pairs={{0,1},{2,3},{4,5},{6,7},{8,9},{10,11},{12,13},{14,15},{1,0},{3,2},... | collective-permute-start | bytes 491528 | tf_op jit(solution)/shard_map/ppermute | solution.py:615
  18.1 6.3 %collective-permute-start.2 = (bf16[4,128,128]{2,1,0:T(8,128)(2,1)S(1)}, bf16[4,128,128]{2,1,0:T(8,128)(2,1)S(1)}, u32[]{:S(2)}, u32[]{:S(2)}) collective-permute-start(bf16[4,128,128]{2,1,0:T(8,128)(2,1)S(1)} %get-tuple-element.25), channel_id=1, source_target_pairs={{1,2},{3,4},{5,6},{7,8},{9,10},{11,12},{13,14},{2,1},{4,3},{6,5},{... | collective-permute-start | bytes 393224 | tf_op jit(solution)/shard_map/ppermute | solution.py:621
where the time goes:
time: 24.7 us; the launch traced here: 25.2 us
  Pallas kernels  10.3 us (42%)
  starting transfers between devices  9.75 us (39%)
  waiting for transfers between devices  4.98 us (20%)
    ppermute x3, starting transfers between devices, to_second(): got = lax.ppermute(x, 'blk', pairs + [(j, i) for i, j in pairs])  7.81 us
    ppermute x3, waiting for transfers between devices, to_second(): got = lax.ppermute(x, 'blk', pairs + [(j, i) for i, j in pairs])  4.97 us
    pallas_call x1, Pallas kernels, local(): call(functools.partial(near_kernel, geo), (acc_type, pack(geo.early)) + t...  3.13 us
    pallas_call x1, Pallas kernels, local(): call(functools.partial(inner_kernel, geo), (acc_type, whole), [SMEM_SPEC]...  2.12 us
    ppermute x3, starting transfers between devices, to_first(): got = lax.ppermute(x, 'blk', pairs + [(j, i) for i, j in pairs])  1.95 us
    pallas_call x2, Pallas kernels, local(): call(functools.partial(kernel_of, geo), whole, [SMEM_SPEC] + [VMEM_SPEC]...  1.63 us
    pallas_call x1, Pallas kernels, local(): call(functools.partial(pack_kernel, geo), (pack(geo.halo),) * 2 + (pltpu....  1.43 us
    pallas_call x1, Pallas kernels, local(): call(functools.partial(early_kernel, geo), acc_type, [SMEM_SPEC] + [VMEM_...  1.22 us
  transfers between devices with their start and end apart: 6, of which 2 were waited for; matrix products, arithmetic and copies ran while one was open for 0% of the time, Pallas kernels for 32%

commit v1 on v0

--- a/solution.py
+++ b/solution.py
@@ -11,8 +11,8 @@
 GROUP = 2
 LATE_GROUP = 4
 LISTS = 7
-BUDGET = 44
-WAIT = (18, 20)
+BUDGET = 41
+WAIT = 18
 COST = (10, 7)
 SMEM_SPEC = pl.BlockSpec(memory_space=pltpu.SMEM)
 VMEM_SPEC = pl.BlockSpec(memory_space=pltpu.VMEM)
@@ -171,28 +171,31 @@
 
 def pack_kernel(
     geo, density_ref, centre_in, offsets_in, counts_in,
-    near_ref, cross_ref, meta_ref, acc_ref,
+    near_a, near_b, cross_ref, meta_ref, acc_ref,
     centre_ref, offsets_ref, counts_ref, sems,
 ):
     index = lax.axis_index("blk")
     odd = index % 2 == 1
 
     def copies(up, down):
+        near = 0 if up else 1
+        parts = [(cross_ref, geo.packs[1 - near])]
+        parts += [(ref, geo.near_packs(i)[near]) for i, ref in enumerate((near_a, near_b))]
         return [
             pltpu.make_async_copy(
                 density_ref.at[pl.ds(start, count)], ref.at[pl.ds(place, count)], sems.at[side, i]
             )
-            for side, (pack, ref) in enumerate(zip(geo.packs, (up, down)))
+            for side, (ref, pack) in enumerate(parts)
             for i, (start, place, count) in enumerate(pack)
         ]
 
-    def start(up, down):
+    def act(up, down, what):
         for copy in copies(up, down):
-            copy.start()
-
-    by_parity(odd, start, near_ref, cross_ref)
+            what(copy)
+
+    by_parity(odd, lambda up, down: act(up, down, lambda c: c.start()), True, False)
     scalars = [
-        pltpu.make_async_copy(*pair, sems.at[2, i])
+        pltpu.make_async_copy(*pair, sems.at[3, i])
         for i, pair in enumerate(
             ((centre_in, centre_ref), (offsets_in, offsets_ref), (counts_in, counts_ref))
         )
@@ -204,8 +207,7 @@
     for copy in scalars:
         copy.wait()
     build_lists(geo, index, centre_ref, offsets_ref, counts_ref, meta_ref)
-    for copy in copies(near_ref, cross_ref):
-        copy.wait()
+    by_parity(odd, lambda up, down: act(up, down, lambda c: c.wait()), True, False)
 
 
 def group_count(geo, meta_ref, which):
@@ -220,8 +222,8 @@
     before = BUDGET
     for which in (CROSS_MANY, CROSS_FEW, NEAR_MANY, NEAR_FEW):
         before = before - COST[which % 2] * group_count(geo, meta_ref, which)
-    odd = meta_ref[geo.odd_at] == 1
-    waiting = jnp.where(waits(), jnp.where(odd, WAIT[1], WAIT[0]), 0)
+    rounds = (meta_ref[geo.lengths_at + CROSS] + LATE_GROUP - 1) // LATE_GROUP
+    waiting = jnp.where(waits(), WAIT - COST[0] * jnp.maximum(rounds - 1, 0), 0)
     share = []
     for which in (INNER_MANY, INNER_FEW):
         cost, count = COST[which % 2], group_count(geo, meta_ref, which)
@@ -467,9 +469,12 @@
 
 
 def near_kernel(
-    geo, meta_ref, halo_ref, tiles_ref, ao_ref, kernel_ref, weights_ref, acc_in, acc_ref,
-    early_out, *outs,
+    geo, meta_ref, halo_a, halo_b, tiles_ref, ao_ref, kernel_ref, weights_ref, acc_in, acc_ref,
+    early_out, out_a, out_b, halo_ref,
 ):
+    outs = (out_a, out_b)
+    for ref, (start, count) in zip((halo_a, halo_b), geo.pieces):
+        halo_ref[pl.ds(start, count)] = ref[...]
     early_out[...] = acc_ref[pl.ds(geo.early_at, geo.early)].astype(early_out.dtype)
     refs = (meta_ref, tiles_ref, ao_ref, kernel_ref, weights_ref, acc_ref, halo_ref)
     for which, width in ((NEAR_MANY, geo.slots), (NEAR_FEW, 2)):
@@ -633,21 +638,22 @@
     dma = pltpu.SemaphoreType.DMA
     acc_type = pltpu.VMEM((geo.spare + 1, nb, nb), jnp.float32)
 
-    near_halo, cross_halo, meta, acc = call(
+    pieces = tuple(pack(count) for _, count in geo.pieces)
+    *near_halo, cross_halo, meta, acc = call(
         functools.partial(pack_kernel, geo),
-        (pack(geo.halo),) * 2 + (pltpu.SMEM((geo.meta_size,), jnp.int32), acc_type),
+        pieces + (pack(geo.halo),) + (pltpu.SMEM((geo.meta_size,), jnp.int32), acc_type),
         [ANY_SPEC] * 4,
-        (VMEM_SPEC,) * 2 + (SMEM_SPEC, VMEM_SPEC),
+        (VMEM_SPEC,) * 3 + (SMEM_SPEC, VMEM_SPEC),
         [
             pltpu.SMEM((batches,), jnp.int32),
             pltpu.SMEM((slots, batches), jnp.int32),
             pltpu.SMEM((batches,), jnp.int32),
-            dma((3, max(geo.reach, 3))),
+            dma((4, max(2 * geo.reach, 3))),
         ],
         cost=pl.CostEstimate(flops=10**10, bytes_accessed=10**8, transcendentals=0),
     )(in_hbm(tiles), in_hbm(centre), in_hbm(sig_offsets.T), in_hbm(counts))
     cross_halo = to_second(cross_halo, size)
-    near_halo = to_first(near_halo, size)
+    near_halo = [to_first(piece, size) for piece in near_halo]
 
     panel = (tiles, ao_values, kernel, grid_weights)
     acc = call(
@@ -661,12 +667,12 @@
 
     acc, early, *first = call(
         functools.partial(near_kernel, geo),
-        (acc_type, pack(geo.early)) + tuple(pack(count) for _, count in geo.pieces),
-        [SMEM_SPEC] + [VMEM_SPEC] * 6,
+        (acc_type, pack(geo.early)) + pieces,
+        [SMEM_SPEC] + [VMEM_SPEC] * 7,
         (VMEM_SPEC,) * 4,
-        [],
-        {6: 0},
-    )(meta, near_halo, *panel, acc)
+        [pack(geo.halo)],
+        {7: 0},
+    )(meta, *near_halo, *panel, acc)
     early = to_second(early, size)
     first = [to_first(piece, size) for piece in first]
 

time: 24.7 us -> 24.9 us (level)
  the two profiles are of different devices: /device:TPU:19 before, /device:TPU:14 now
where the time goes in v1:
time: 24.9 us; the launch traced here: 24.6 us
  Pallas kernels  11.8 us (47%)
  starting transfers between devices  10.1 us (41%)
  waiting for transfers between devices  2.55 us (10%)
    ppermute x3, starting transfers between devices, to_second(): got = lax.ppermute(x, 'blk', pairs + [(j, i) for i, j in pairs])  6.66 us
    ppermute x4, starting transfers between devices, to_first(): got = lax.ppermute(x, 'blk', pairs + [(j, i) for i, j in pairs])  3.45 us
    pallas_call x1, Pallas kernels, local(): call(functools.partial(inner_kernel, geo), (acc_type, whole), [SMEM_SPEC]...  2.76 us
    ppermute x3, waiting for transfers between devices, to_second(): got = lax.ppermute(x, 'blk', pairs + [(j, i) for i, j in pairs])  2.54 us
    pallas_call x1, Pallas kernels, local(): call(functools.partial(near_kernel, geo), (acc_type, pack(geo.early)) + p...  2.37 us
    pallas_call x1, Pallas kernels, local(): call(functools.partial(early_kernel, geo), acc_type, [SMEM_SPEC] + [VMEM_...  1.82 us
    pallas_call x1, Pallas kernels, local(): call(functools.partial(waiting_kernel, geo), (acc_type, pltpu.SMEM((1,),...  1.6 us
    pallas_call x1, Pallas kernels, local(): call(functools.partial(pack_kernel, geo), pieces + (pack(geo.halo),) + (p...  1.49 us
  transfers between devices with their start and end apart: 7, of which 1 were waited for; matrix products, arithmetic and copies ran while one was open for 0% of the time, Pallas kernels for 38%

profile of v1, /device:TPU:14, one launch (start us, length us, event | category | flops | bytes accessed | tf_op | source)
XLA Modules:
  0.0 24.6 jit_solution(10904973688749109472)
XLA Ops:
  0.0 0.0 copy-start
  0.0 0.0 copy-start.1
  0.0 0.0 copy-start.2
  0.0 0.0 copy-start.3
  0.0 1.5 %shard_map.73 = (bf16[6,128,128]{2,1,0:T(8,128)(2,1)S(1)}, bf16[5,128,128]{2,1,0:T(8,128)(2,1)S(1)}, bf16[11,128,128]{2,1,0:T(8,128)(2,1)S(1)}, s32[178]{0:T(256)S(4)}, f32[91,128,128]{2,1,0:T(8,128)S(1)}) custom-call(bf16[72,128,128]{2,1,0:T(8,128)(2,1)} %bitcast.3, s32[12]{0:T(128)} %centre_in.1, s32[4,12]{1,0:T(4,128)} %bitcast.8, s32[12]{0:T(128)} %counts_in.1), custom_call_target="tpu_custom_call" | custom-call | flops 10000000000 | bytes 100000000 | tf_op jit(solution)/shard_map/pallas_call | solution.py:642
  1.5 2.2 %collective-permute-start.2 = (bf16[11,128,128]{2,1,0:T(8,128)(2,1)S(1)}, bf16[11,128,128]{2,1,0:T(8,128)(2,1)S(1)}, u32[]{:S(2)}, u32[]{:S(2)}) collective-permute-start(bf16[11,128,128]{2,1,0:T(8,128)(2,1)S(1)} %get-tuple-element.26), channel_id=1, source_target_pairs={{1,2},{3,4},{5,6},{7,8},{9,10},{11,12},{13,14},{2,1},{4,3},{6,5},{... | collective-permute-start | bytes 1081352 | tf_op jit(solution)/shard_map/ppermute | solution.py:626
  3.7 1.7 %collective-permute-start = (bf16[6,128,128]{2,1,0:T(8,128)(2,1)S(1)}, bf16[6,128,128]{2,1,0:T(8,128)(2,1)S(1)}, u32[]{:S(2)}, u32[]{:S(2)}) collective-permute-start(bf16[6,128,128]{2,1,0:T(8,128)(2,1)S(1)} %get-tuple-element.21), channel_id=1, source_target_pairs={{0,1},{2,3},{4,5},{6,7},{8,9},{10,11},{12,13},{14,15},{1,0},{3,2},... | collective-permute-start | bytes 589832 | tf_op jit(solution)/shard_map/ppermute | solution.py:620
  5.4 0.1 collective-permute-start.1
  5.5 0.0 copy-done
  5.5 0.0 copy-done.1
  5.5 0.0 copy-done.2
  5.5 0.0 copy-done.3
  5.5 1.8 %shard_map.74.acc_in = f32[91,128,128]{2,1,0:T(8,128)S(1)} custom-call(s32[178]{0:T(256)S(4)} %get-tuple-element.20.meta_ref, bf16[72,128,128]{2,1,0:T(8,128)(2,1)S(1)} %bitcast.4, bf16[12,4,128,256]{3,2,1,0:T(8,128)(2,1)S(1)} %copy-done, bf16[12,256,256]{2,1,0:T(8,128)(2,1)S(1)} %copy-done.1, ...), custom_call_target="tpu_custom_call", output_to_operand_aliasing={{}: (5, {})} | custom-call | tf_op jit(solution)/shard_map/pallas_call | solution.py:659
  7.3 0.0 collective-permute-done.1.halo_b
  7.3 0.0 collective-permute-done.halo_a
  7.3 2.4 %shard_map.75 = (f32[91,128,128]{2,1,0:T(8,128)S(1)}, bf16[7,128,128]{2,1,0:T(8,128)(2,1)S(1)}, bf16[6,128,128]{2,1,0:T(8,128)(2,1)S(1)}, bf16[5,128,128]{2,1,0:T(8,128)(2,1)S(1)}) custom-call(s32[178]{0:T(256)S(4)} %get-tuple-element.20.meta_ref, bf16[6,128,128]{2,1,0:T(8,128)(2,1)S(1)} %collective-permute-done.halo_a, ...), custom_call_target="tpu_custom_call", output_to_operand_aliasing={{0}: (7, {})} | custom-call | tf_op jit(solution)/shard_map/pallas_call | solution.py:668
  9.7 2.2 %collective-permute-start.4 = (bf16[7,128,128]{2,1,0:T(8,128)(2,1)S(1)}, bf16[7,128,128]{2,1,0:T(8,128)(2,1)S(1)}, u32[]{:S(2)}, u32[]{:S(2)}) collective-permute-start(bf16[7,128,128]{2,1,0:T(8,128)(2,1)S(1)} %get-tuple-element.28), channel_id=1, source_target_pairs={{1,2},{3,4},{5,6},{7,8},{9,10},{11,12},{13,14},{2,1},{4,3},{6,5},{... | collective-permute-start | bytes 688136 | tf_op jit(solution)/shard_map/ppermute | solution.py:626
  11.9 1.6 %collective-permute-start.5 = (bf16[6,128,128]{2,1,0:T(8,128)(2,1)S(1)}, bf16[6,128,128]{2,1,0:T(8,128)(2,1)S(1)}, u32[]{:S(2)}, u32[]{:S(2)}) collective-permute-start(bf16[6,128,128]{2,1,0:T(8,128)(2,1)S(1)} %get-tuple-element.29), channel_id=1, source_target_pairs={{0,1},{2,3},{4,5},{6,7},{8,9},{10,11},{12,13},{14,15},{1,0},{3,2},... | collective-permute-start | bytes 589832 | tf_op jit(solution)/shard_map/ppermute | solution.py:620
  13.6 0.1 collective-permute-start.6
  13.6 1.6 %shard_map.76 = (f32[91,128,128]{2,1,0:T(8,128)S(1)}, s32[1]{0:T(128)S(4)}) custom-call(s32[178]{0:T(256)S(4)} %get-tuple-element.20.meta_ref, bf16[72,128,128]{2,1,0:T(8,128)(2,1)S(1)} %bitcast.6, bf16[12,4,128,256]{3,2,1,0:T(8,128)(2,1)S(1)} %copy-done, bf16[12,256,256]{2,1,0:T(8,128)(2,1)S(1)} %copy-done.1, ...), custom_call_target="tpu_custom_call", output_to_operand_aliasing={{0}: (5, {})} | custom-call | tf_op jit(solution)/shard_map/pallas_call | solution.py:679
  15.2 0.0 collective-permute-done.2.halo_ref
  15.2 0.7 %shard_map.77 = (bf16[13,256,256]{2,1,0:T(8,128)(2,1)S(1)}, bf16[4,128,128]{2,1,0:T(8,128)(2,1)S(1)}) custom-call(s32[178]{0:T(256)S(4)} %get-tuple-element.20.meta_ref, s32[1]{0:T(128)S(4)} %get-tuple-element.25.done_ref, bf16[11,128,128]{2,1,0:T(8,128)(2,1)S(1)} %collective-permute-done.2.halo_ref, bf16[12,4,128,256]{3,2,1,0:T(8,128)(2,1)S(1)} %copy-done, ...), custom_call_target="tpu_custom_call" | custom-call | tf_op jit(solution)/shard_map/pallas_call | solution.py:689
  16.0 2.2 %collective-permute-start.3 = (bf16[4,128,128]{2,1,0:T(8,128)(2,1)S(1)}, bf16[4,128,128]{2,1,0:T(8,128)(2,1)S(1)}, u32[]{:S(2)}, u32[]{:S(2)}) collective-permute-start(bf16[4,128,128]{2,1,0:T(8,128)(2,1)S(1)} %get-tuple-element.27), channel_id=1, source_target_pairs={{1,2},{3,4},{5,6},{7,8},{9,10},{11,12},{13,14},{2,1},{4,3},{6,5},{... | collective-permute-start | bytes 393224 | tf_op jit(solution)/shard_map/ppermute | solution.py:626
  18.3 0.0 collective-permute-done.6.first_b
  18.3 0.0 collective-permute-done.5.first_a
  18.3 2.8 %shard_map.78 = (f32[91,128,128]{2,1,0:T(8,128)S(1)}, f32[72,128,128]{2,1,0:T(8,128)}) custom-call(s32[178]{0:T(256)S(4)} %get-tuple-element.20.meta_ref, bf16[6,128,128]{2,1,0:T(8,128)(2,1)S(1)} %collective-permute-done.5.first_a, bf16[5,128,128]{2,1,0:T(8,128)(2,1)S(1)} %collective-permute-done.6.first_b, ...), custom_call_target="tpu_custom_call", output_to_operand_aliasing={{0}: (8, {})} | custom-call | tf_op jit(solution)/shard_map/pallas_call | solution.py:699
  21.0 0.0 collective-permute-done.4.early_ref
  21.0 0.1 shard_map.79.out_in
  21.2 2.5 %collective-permute-done.3.late_ref = bf16[4,128,128]{2,1,0:T(8,128)(2,1)S(1)} collective-permute-done((bf16[4,128,128]{2,1,0:T(8,128)(2,1)S(1)}, bf16[4,128,128]{2,1,0:T(8,128)(2,1)S(1)}, u32[]{:S(2)}, u32[]{:S(2)}) %collective-permute-start.3) | collective-permute-done | bytes 131104 | tf_op jit(solution)/shard_map/ppermute | solution.py:626
  23.7 0.9 %shard_map.80 = f32[72,128,128]{2,1,0:T(8,128)} custom-call(s32[178]{0:T(256)S(4)} %get-tuple-element.20.meta_ref, bf16[4,128,128]{2,1,0:T(8,128)(2,1)S(1)} %collective-permute-done.3.late_ref, bf16[7,128,128]{2,1,0:T(8,128)(2,1)S(1)} %collective-permute-done.4.early_ref, ...), custom_call_target="tpu_custom_call", output_to_operand_aliasing={{}: (4, {})} | custom-call | tf_op jit(solution)/shard_map/pallas_call | solution.py:712
Async XLA Ops:
  0.0 5.5 %copy-start = (bf16[12,4,128,256]{3,2,1,0:T(8,128)(2,1)S(1)}, bf16[12,4,128,256]{3,2,1,0:T(8,128)(2,1)}, u32[]{:S(2)}) copy-start(bf16[12,4,128,256]{3,2,1,0:T(8,128)(2,1)} %ao_ref.9) | copy-start | bytes 9437188
  0.0 5.5 %copy-start.1 = (bf16[12,256,256]{2,1,0:T(8,128)(2,1)S(1)}, bf16[12,256,256]{2,1,0:T(8,128)(2,1)}, u32[]{:S(2)}) copy-start(bf16[12,256,256]{2,1,0:T(8,128)(2,1)} %kernel_ref.9) | copy-start | bytes 4718596
  0.0 5.5 %copy-start.2 = (bf16[8,9,128,128]{3,2,1,0:T(8,128)(2,1)S(1)}, bf16[8,9,128,128]{3,2,1,0:T(8,128)(2,1)}, u32[]{:S(2)}) copy-start(bf16[8,9,128,128]{3,2,1,0:T(8,128)(2,1)} %param.7) | copy-start | bytes 7077892
  0.0 5.5 %copy-start.3 = (f32[12,256]{1,0:T(8,128)S(1)}, f32[12,256]{1,0:T(8,128)}, u32[]{:S(2)}) copy-start(f32[12,256]{1,0:T(8,128)} %weights_ref.9) | copy-start | bytes 36868
  1.5 13.7 %collective-permute-start.2 = (bf16[11,128,128]{2,1,0:T(8,128)(2,1)S(1)}, bf16[11,128,128]{2,1,0:T(8,128)(2,1)S(1)}, u32[]{:S(2)}, u32[]{:S(2)}) collective-permute-start(bf16[11,128,128]{2,1,0:T(8,128)(2,1)S(1)} %get-tuple-element.26), channel_id=1, source_target_pairs={{1,2},{3,4},{5,6},{7,8},{9,10},{11,12},{13,14},{2,1},{4,3},{6,5},{... | collective-permute-start | bytes 1081352 | tf_op jit(solution)/shard_map/ppermute | solution.py:626
  3.7 3.6 %collective-permute-start = (bf16[6,128,128]{2,1,0:T(8,128)(2,1)S(1)}, bf16[6,128,128]{2,1,0:T(8,128)(2,1)S(1)}, u32[]{:S(2)}, u32[]{:S(2)}) collective-permute-start(bf16[6,128,128]{2,1,0:T(8,128)(2,1)S(1)} %get-tuple-element.21), channel_id=1, source_target_pairs={{0,1},{2,3},{4,5},{6,7},{8,9},{10,11},{12,13},{14,15},{1,0},{3,2},... | collective-permute-start | bytes 589832 | tf_op jit(solution)/shard_map/ppermute | solution.py:620
  5.4 1.9 %collective-permute-start.1 = (bf16[5,128,128]{2,1,0:T(8,128)(2,1)S(1)}, bf16[5,128,128]{2,1,0:T(8,128)(2,1)S(1)}, u32[]{:S(2)}, u32[]{:S(2)}) collective-permute-start(bf16[5,128,128]{2,1,0:T(8,128)(2,1)S(1)} %get-tuple-element.22), channel_id=1, source_target_pairs={{0,1},{2,3},{4,5},{6,7},{8,9},{10,11},{12,13},{14,15},{1,0},{3,2},... | collective-permute-start | bytes 491528 | tf_op jit(solution)/shard_map/ppermute | solution.py:620
  9.7 11.3 %collective-permute-start.4 = (bf16[7,128,128]{2,1,0:T(8,128)(2,1)S(1)}, bf16[7,128,128]{2,1,0:T(8,128)(2,1)S(1)}, u32[]{:S(2)}, u32[]{:S(2)}) collective-permute-start(bf16[7,128,128]{2,1,0:T(8,128)(2,1)S(1)} %get-tuple-element.28), channel_id=1, source_target_pairs={{1,2},{3,4},{5,6},{7,8},{9,10},{11,12},{13,14},{2,1},{4,3},{6,5},{... | collective-permute-start | bytes 688136 | tf_op jit(solution)/shard_map/ppermute | solution.py:626
  11.9 6.3 %collective-permute-start.5 = (bf16[6,128,128]{2,1,0:T(8,128)(2,1)S(1)}, bf16[6,128,128]{2,1,0:T(8,128)(2,1)S(1)}, u32[]{:S(2)}, u32[]{:S(2)}) collective-permute-start(bf16[6,128,128]{2,1,0:T(8,128)(2,1)S(1)} %get-tuple-element.29), channel_id=1, source_target_pairs={{0,1},{2,3},{4,5},{6,7},{8,9},{10,11},{12,13},{14,15},{1,0},{3,2},... | collective-permute-start | bytes 589832 | tf_op jit(solution)/shard_map/ppermute | solution.py:620
  13.6 4.7 %collective-permute-start.6 = (bf16[5,128,128]{2,1,0:T(8,128)(2,1)S(1)}, bf16[5,128,128]{2,1,0:T(8,128)(2,1)S(1)}, u32[]{:S(2)}, u32[]{:S(2)}) collective-permute-start(bf16[5,128,128]{2,1,0:T(8,128)(2,1)S(1)} %get-tuple-element.30), channel_id=1, source_target_pairs={{0,1},{2,3},{4,5},{6,7},{8,9},{10,11},{12,13},{14,15},{1,0},{3,2},... | collective-permute-start | bytes 491528 | tf_op jit(solution)/shard_map/ppermute | solution.py:620
  16.0 7.7 %collective-permute-start.3 = (bf16[4,128,128]{2,1,0:T(8,128)(2,1)S(1)}, bf16[4,128,128]{2,1,0:T(8,128)(2,1)S(1)}, u32[]{:S(2)}, u32[]{:S(2)}) collective-permute-start(bf16[4,128,128]{2,1,0:T(8,128)(2,1)S(1)} %get-tuple-element.27), channel_id=1, source_target_pairs={{1,2},{3,4},{5,6},{7,8},{9,10},{11,12},{13,14},{2,1},{4,3},{6,5},{... | collective-permute-start | bytes 393224 | tf_op jit(solution)/shard_map/ppermute | solution.py:626

commit v2 on v1

--- a/solution.py
+++ b/solution.py
@@ -12,7 +12,7 @@
 LATE_GROUP = 4
 LISTS = 7
 BUDGET = 41
-WAIT = 18
+WAIT = 8
 COST = (10, 7)
 SMEM_SPEC = pl.BlockSpec(memory_space=pltpu.SMEM)
 VMEM_SPEC = pl.BlockSpec(memory_space=pltpu.VMEM)

time: 24.9 us -> 24.5 us (0.984)
  the two profiles are of different devices: /device:TPU:14 before, /device:TPU:9 now
where the time goes in v2:
time: 24.5 us; the launch traced here: 24 us
  starting transfers between devices  11.9 us (49%)
  Pallas kernels  10.5 us (43%)
  waiting for transfers between devices  1.4 us (6%)
    ppermute x3, starting transfers between devices, to_second(): got = lax.ppermute(x, 'blk', pairs + [(j, i) for i, j in pairs])  10.5 us
    pallas_call x1, Pallas kernels, local(): call(functools.partial(near_kernel, geo), (acc_type, pack(geo.early)) + p...  2.76 us
    pallas_call x1, Pallas kernels, local(): call(functools.partial(inner_kernel, geo), (acc_type, whole), [SMEM_SPEC]...  2.74 us
    pallas_call x1, Pallas kernels, local(): call(functools.partial(pack_kernel, geo), pieces + (pack(geo.halo),) + (p...  1.49 us
    ppermute x4, starting transfers between devices, to_first(): got = lax.ppermute(x, 'blk', pairs + [(j, i) for i, j in pairs])  1.4 us
    ppermute x3, waiting for transfers between devices, to_second(): got = lax.ppermute(x, 'blk', pairs + [(j, i) for i, j in pairs])  1.39 us
    pallas_call x1, Pallas kernels, local(): call(functools.partial(early_kernel, geo), acc_type, [SMEM_SPEC] + [VMEM_...  1.21 us
    pallas_call x2, Pallas kernels, local(): call(functools.partial(kernel_of, geo), whole, [SMEM_SPEC] + [VMEM_SPEC]...  1 us
  transfers between devices with their start and end apart: 7, of which 1 were waited for; matrix products, arithmetic and copies ran while one was open for 0% of the time, Pallas kernels for 34%

profile of v2, /device:TPU:9, one launch (start us, length us, event | category | flops | bytes accessed | tf_op | source)
XLA Modules:
  0.0 24.0 jit_solution(11227086049042524664)
XLA Ops:
  0.0 0.0 copy-start
  0.0 0.0 copy-start.1
  0.0 0.0 copy-start.2
  0.0 0.0 copy-start.3
  0.0 1.5 %shard_map.73 = (bf16[6,128,128]{2,1,0:T(8,128)(2,1)S(1)}, bf16[5,128,128]{2,1,0:T(8,128)(2,1)S(1)}, bf16[11,128,128]{2,1,0:T(8,128)(2,1)S(1)}, s32[178]{0:T(256)S(4)}, f32[91,128,128]{2,1,0:T(8,128)S(1)}) custom-call(bf16[72,128,128]{2,1,0:T(8,128)(2,1)} %bitcast.3, s32[12]{0:T(128)} %centre_in.1, s32[4,12]{1,0:T(4,128)} %bitcast.8, s32[12]{0:T(128)} %counts_in.1), custom_call_target="tpu_custom_call" | custom-call | flops 10000000000 | bytes 100000000 | tf_op jit(solution)/shard_map/pallas_call | solution.py:642
  1.5 4.0 %collective-permute-start.2 = (bf16[11,128,128]{2,1,0:T(8,128)(2,1)S(1)}, bf16[11,128,128]{2,1,0:T(8,128)(2,1)S(1)}, u32[]{:S(2)}, u32[]{:S(2)}) collective-permute-start(bf16[11,128,128]{2,1,0:T(8,128)(2,1)S(1)} %get-tuple-element.26), channel_id=1, source_target_pairs={{1,2},{3,4},{5,6},{7,8},{9,10},{11,12},{13,14},{2,1},{4,3},{6,5},{... | collective-permute-start | bytes 1081352 | tf_op jit(solution)/shard_map/ppermute | solution.py:626
  5.5 0.1 collective-permute-start
  5.6 0.5 %collective-permute-start.1 = (bf16[5,128,128]{2,1,0:T(8,128)(2,1)S(1)}, bf16[5,128,128]{2,1,0:T(8,128)(2,1)S(1)}, u32[]{:S(2)}, u32[]{:S(2)}) collective-permute-start(bf16[5,128,128]{2,1,0:T(8,128)(2,1)S(1)} %get-tuple-element.22), channel_id=1, source_target_pairs={{0,1},{2,3},{4,5},{6,7},{8,9},{10,11},{12,13},{14,15},{1,0},{3,2},... | collective-permute-start | bytes 491528 | tf_op jit(solution)/shard_map/ppermute | solution.py:620
  6.1 0.0 copy-done
  6.1 0.0 copy-done.1
  6.1 0.0 copy-done.2
  6.1 0.0 copy-done.3
  6.1 1.2 %shard_map.74.acc_in = f32[91,128,128]{2,1,0:T(8,128)S(1)} custom-call(s32[178]{0:T(256)S(4)} %get-tuple-element.20.meta_ref, bf16[72,128,128]{2,1,0:T(8,128)(2,1)S(1)} %bitcast.4, bf16[12,4,128,256]{3,2,1,0:T(8,128)(2,1)S(1)} %copy-done, bf16[12,256,256]{2,1,0:T(8,128)(2,1)S(1)} %copy-done.1, ...), custom_call_target="tpu_custom_call", output_to_operand_aliasing={{}: (5, {})} | custom-call | tf_op jit(solution)/shard_map/pallas_call | solution.py:659
  7.3 0.0 collective-permute-done.1.halo_b
  7.3 0.0 collective-permute-done.halo_a
  7.3 2.8 %shard_map.75 = (f32[91,128,128]{2,1,0:T(8,128)S(1)}, bf16[7,128,128]{2,1,0:T(8,128)(2,1)S(1)}, bf16[6,128,128]{2,1,0:T(8,128)(2,1)S(1)}, bf16[5,128,128]{2,1,0:T(8,128)(2,1)S(1)}) custom-call(s32[178]{0:T(256)S(4)} %get-tuple-element.20.meta_ref, bf16[6,128,128]{2,1,0:T(8,128)(2,1)S(1)} %collective-permute-done.halo_a, ...), custom_call_target="tpu_custom_call", output_to_operand_aliasing={{0}: (7, {})} | custom-call | tf_op jit(solution)/shard_map/pallas_call | solution.py:668
  10.1 3.1 %collective-permute-start.4 = (bf16[7,128,128]{2,1,0:T(8,128)(2,1)S(1)}, bf16[7,128,128]{2,1,0:T(8,128)(2,1)S(1)}, u32[]{:S(2)}, u32[]{:S(2)}) collective-permute-start(bf16[7,128,128]{2,1,0:T(8,128)(2,1)S(1)} %get-tuple-element.28), channel_id=1, source_target_pairs={{1,2},{3,4},{5,6},{7,8},{9,10},{11,12},{13,14},{2,1},{4,3},{6,5},{... | collective-permute-start | bytes 688136 | tf_op jit(solution)/shard_map/ppermute | solution.py:626
  13.2 0.8 %collective-permute-start.5 = (bf16[6,128,128]{2,1,0:T(8,128)(2,1)S(1)}, bf16[6,128,128]{2,1,0:T(8,128)(2,1)S(1)}, u32[]{:S(2)}, u32[]{:S(2)}) collective-permute-start(bf16[6,128,128]{2,1,0:T(8,128)(2,1)S(1)} %get-tuple-element.29), channel_id=1, source_target_pairs={{0,1},{2,3},{4,5},{6,7},{8,9},{10,11},{12,13},{14,15},{1,0},{3,2},... | collective-permute-start | bytes 589832 | tf_op jit(solution)/shard_map/ppermute | solution.py:620
  14.0 0.1 collective-permute-start.6
  14.1 0.6 %shard_map.76 = (f32[91,128,128]{2,1,0:T(8,128)S(1)}, s32[1]{0:T(128)S(4)}) custom-call(s32[178]{0:T(256)S(4)} %get-tuple-element.20.meta_ref, bf16[72,128,128]{2,1,0:T(8,128)(2,1)S(1)} %bitcast.6, bf16[12,4,128,256]{3,2,1,0:T(8,128)(2,1)S(1)} %copy-done, bf16[12,256,256]{2,1,0:T(8,128)(2,1)S(1)} %copy-done.1, ...), custom_call_target="tpu_custom_call", output_to_operand_aliasing={{0}: (5, {})} | custom-call | tf_op jit(solution)/shard_map/pallas_call | solution.py:679
  14.7 0.0 collective-permute-done.2.halo_ref
  14.7 0.8 %shard_map.77 = (bf16[13,256,256]{2,1,0:T(8,128)(2,1)S(1)}, bf16[4,128,128]{2,1,0:T(8,128)(2,1)S(1)}) custom-call(s32[178]{0:T(256)S(4)} %get-tuple-element.20.meta_ref, s32[1]{0:T(128)S(4)} %get-tuple-element.25.done_ref, bf16[11,128,128]{2,1,0:T(8,128)(2,1)S(1)} %collective-permute-done.2.halo_ref, bf16[12,4,128,256]{3,2,1,0:T(8,128)(2,1)S(1)} %copy-done, ...), custom_call_target="tpu_custom_call" | custom-call | tf_op jit(solution)/shard_map/pallas_call | solution.py:689
  15.4 3.4 %collective-permute-start.3 = (bf16[4,128,128]{2,1,0:T(8,128)(2,1)S(1)}, bf16[4,128,128]{2,1,0:T(8,128)(2,1)S(1)}, u32[]{:S(2)}, u32[]{:S(2)}) collective-permute-start(bf16[4,128,128]{2,1,0:T(8,128)(2,1)S(1)} %get-tuple-element.27), channel_id=1, source_target_pairs={{1,2},{3,4},{5,6},{7,8},{9,10},{11,12},{13,14},{2,1},{4,3},{6,5},{... | collective-permute-start | bytes 393224 | tf_op jit(solution)/shard_map/ppermute | solution.py:626
  18.9 0.0 collective-permute-done.6.first_b
  18.9 0.0 collective-permute-done.5.first_a
  18.9 2.7 %shard_map.78 = (f32[91,128,128]{2,1,0:T(8,128)S(1)}, f32[72,128,128]{2,1,0:T(8,128)}) custom-call(s32[178]{0:T(256)S(4)} %get-tuple-element.20.meta_ref, bf16[6,128,128]{2,1,0:T(8,128)(2,1)S(1)} %collective-permute-done.5.first_a, bf16[5,128,128]{2,1,0:T(8,128)(2,1)S(1)} %collective-permute-done.6.first_b, ...), custom_call_target="tpu_custom_call", output_to_operand_aliasing={{0}: (8, {})} | custom-call | tf_op jit(solution)/shard_map/pallas_call | solution.py:699
  21.6 0.0 collective-permute-done.4.early_ref
  21.6 0.1 shard_map.79.out_in
  21.7 1.4 %collective-permute-done.3.late_ref = bf16[4,128,128]{2,1,0:T(8,128)(2,1)S(1)} collective-permute-done((bf16[4,128,128]{2,1,0:T(8,128)(2,1)S(1)}, bf16[4,128,128]{2,1,0:T(8,128)(2,1)S(1)}, u32[]{:S(2)}, u32[]{:S(2)}) %collective-permute-start.3) | collective-permute-done | bytes 131104 | tf_op jit(solution)/shard_map/ppermute | solution.py:626
  23.1 0.9 %shard_map.80 = f32[72,128,128]{2,1,0:T(8,128)} custom-call(s32[178]{0:T(256)S(4)} %get-tuple-element.20.meta_ref, bf16[4,128,128]{2,1,0:T(8,128)(2,1)S(1)} %collective-permute-done.3.late_ref, bf16[7,128,128]{2,1,0:T(8,128)(2,1)S(1)} %collective-permute-done.4.early_ref, ...), custom_call_target="tpu_custom_call", output_to_operand_aliasing={{}: (4, {})} | custom-call | tf_op jit(solution)/shard_map/pallas_call | solution.py:712
Async XLA Ops:
  0.0 6.1 %copy-start = (bf16[12,4,128,256]{3,2,1,0:T(8,128)(2,1)S(1)}, bf16[12,4,128,256]{3,2,1,0:T(8,128)(2,1)}, u32[]{:S(2)}) copy-start(bf16[12,4,128,256]{3,2,1,0:T(8,128)(2,1)} %ao_ref.9) | copy-start | bytes 9437188
  0.0 6.1 %copy-start.1 = (bf16[12,256,256]{2,1,0:T(8,128)(2,1)S(1)}, bf16[12,256,256]{2,1,0:T(8,128)(2,1)}, u32[]{:S(2)}) copy-start(bf16[12,256,256]{2,1,0:T(8,128)(2,1)} %kernel_ref.9) | copy-start | bytes 4718596
  0.0 6.1 %copy-start.2 = (bf16[8,9,128,128]{3,2,1,0:T(8,128)(2,1)S(1)}, bf16[8,9,128,128]{3,2,1,0:T(8,128)(2,1)}, u32[]{:S(2)}) copy-start(bf16[8,9,128,128]{3,2,1,0:T(8,128)(2,1)} %param.7) | copy-start | bytes 7077892
  0.0 6.1 %copy-start.3 = (f32[12,256]{1,0:T(8,128)S(1)}, f32[12,256]{1,0:T(8,128)}, u32[]{:S(2)}) copy-start(f32[12,256]{1,0:T(8,128)} %weights_ref.9) | copy-start | bytes 36868
  1.5 13.1 %collective-permute-start.2 = (bf16[11,128,128]{2,1,0:T(8,128)(2,1)S(1)}, bf16[11,128,128]{2,1,0:T(8,128)(2,1)S(1)}, u32[]{:S(2)}, u32[]{:S(2)}) collective-permute-start(bf16[11,128,128]{2,1,0:T(8,128)(2,1)S(1)} %get-tuple-element.26), channel_id=1, source_target_pairs={{1,2},{3,4},{5,6},{7,8},{9,10},{11,12},{13,14},{2,1},{4,3},{6,5},{... | collective-permute-start | bytes 1081352 | tf_op jit(solution)/shard_map/ppermute | solution.py:626
  5.5 1.8 %collective-permute-start = (bf16[6,128,128]{2,1,0:T(8,128)(2,1)S(1)}, bf16[6,128,128]{2,1,0:T(8,128)(2,1)S(1)}, u32[]{:S(2)}, u32[]{:S(2)}) collective-permute-start(bf16[6,128,128]{2,1,0:T(8,128)(2,1)S(1)} %get-tuple-element.21), channel_id=1, source_target_pairs={{0,1},{2,3},{4,5},{6,7},{8,9},{10,11},{12,13},{14,15},{1,0},{3,2},... | collective-permute-start | bytes 589832 | tf_op jit(solution)/shard_map/ppermute | solution.py:620
  5.6 1.7 %collective-permute-start.1 = (bf16[5,128,128]{2,1,0:T(8,128)(2,1)S(1)}, bf16[5,128,128]{2,1,0:T(8,128)(2,1)S(1)}, u32[]{:S(2)}, u32[]{:S(2)}) collective-permute-start(bf16[5,128,128]{2,1,0:T(8,128)(2,1)S(1)} %get-tuple-element.22), channel_id=1, source_target_pairs={{0,1},{2,3},{4,5},{6,7},{8,9},{10,11},{12,13},{14,15},{1,0},{3,2},... | collective-permute-start | bytes 491528 | tf_op jit(solution)/shard_map/ppermute | solution.py:620
  10.1 11.5 %collective-permute-start.4 = (bf16[7,128,128]{2,1,0:T(8,128)(2,1)S(1)}, bf16[7,128,128]{2,1,0:T(8,128)(2,1)S(1)}, u32[]{:S(2)}, u32[]{:S(2)}) collective-permute-start(bf16[7,128,128]{2,1,0:T(8,128)(2,1)S(1)} %get-tuple-element.28), channel_id=1, source_target_pairs={{1,2},{3,4},{5,6},{7,8},{9,10},{11,12},{13,14},{2,1},{4,3},{6,5},{... | collective-permute-start | bytes 688136 | tf_op jit(solution)/shard_map/ppermute | solution.py:626
  13.2 5.6 %collective-permute-start.5 = (bf16[6,128,128]{2,1,0:T(8,128)(2,1)S(1)}, bf16[6,128,128]{2,1,0:T(8,128)(2,1)S(1)}, u32[]{:S(2)}, u32[]{:S(2)}) collective-permute-start(bf16[6,128,128]{2,1,0:T(8,128)(2,1)S(1)} %get-tuple-element.29), channel_id=1, source_target_pairs={{0,1},{2,3},{4,5},{6,7},{8,9},{10,11},{12,13},{14,15},{1,0},{3,2},... | collective-permute-start | bytes 589832 | tf_op jit(solution)/shard_map/ppermute | solution.py:620
  14.0 4.9 %collective-permute-start.6 = (bf16[5,128,128]{2,1,0:T(8,128)(2,1)S(1)}, bf16[5,128,128]{2,1,0:T(8,128)(2,1)S(1)}, u32[]{:S(2)}, u32[]{:S(2)}) collective-permute-start(bf16[5,128,128]{2,1,0:T(8,128)(2,1)S(1)} %get-tuple-element.30), channel_id=1, source_target_pairs={{0,1},{2,3},{4,5},{6,7},{8,9},{10,11},{12,13},{14,15},{1,0},{3,2},... | collective-permute-start | bytes 491528 | tf_op jit(solution)/shard_map/ppermute | solution.py:620
  15.4 7.7 %collective-permute-start.3 = (bf16[4,128,128]{2,1,0:T(8,128)(2,1)S(1)}, bf16[4,128,128]{2,1,0:T(8,128)(2,1)S(1)}, u32[]{:S(2)}, u32[]{:S(2)}) collective-permute-start(bf16[4,128,128]{2,1,0:T(8,128)(2,1)S(1)} %get-tuple-element.27), channel_id=1, source_target_pairs={{1,2},{3,4},{5,6},{7,8},{9,10},{11,12},{13,14},{2,1},{4,3},{6,5},{... | collective-permute-start | bytes 393224 | tf_op jit(solution)/shard_map/ppermute | solution.py:626
